TPU v7x, 512 devices: a whole 4x4x16 slice. The times are simulated.
512 devices in a mesh: occ: 8 (over y, core), vir: 64 (over x, z).
Axes of the slice: x: 4, y: 4, z: 16, core: 2. Of those that a mesh axis runs over, the one named last changes fastest.
Arguments:
- amplitude: float32 [128, 147456], P('occ', 'vir'), may hold values from -6 to 6
- integrals: float32 [8, 64, 64, 32, 128], P('occ', 'vir'), may hold values from -0.03125 to 0.03125
- task_count: int32 [8, 64], P('occ', 'vir'), may hold values from 1 to 64, 2048 in all within a row
- task_owner: int32 [8, 64, 64, 1], P('occ', 'vir'), may hold values from 0 to 63; in each aligned block of 64 rows (0 to 63, 64 to 127, ..., all dimensions but the last counted through in order) at most 2 rows name the same one
- task_local: int32 [8, 64, 64], P('occ', 'vir'), may hold values from 0 to 17
Outputs:
- ladder: float32 [128, 2048], P('occ', 'vir')
Inputs may be any that keep to these rules, and one draw needn't show every extreme that they name: `task_count`: each device has between 1 and 64 live tasks; its live tasks are its first slots, and some device of every index of occ has all 64 live. `task_owner`: among the 64 slots of one device, at most 2 name one index of vir.
All inputs are finite; a program needn't handle non-finite values.
Results may differ from a plain program's by a relative error of at most 0.0003.
Values sent between devices are 32-bit elements; how exact they have to be, the bound alone decides.
A program may use at most 64 MiB of HBM per device.

v0:
```python
import math

import jax
import jax.numpy as jnp
from jax import lax
from jax.sharding import PartitionSpec as P


def accumulate(int_tiles, amp_tiles, live_count):
    slot_count = int_tiles.shape[0]
    group_size = math.gcd(slot_count, 8)
    pair_count = amp_tiles.shape[1]

    def step(block_index, running):
        first = block_index * group_size
        int_block = lax.dynamic_slice_in_dim(int_tiles, first, group_size, 0)
        amp_block = lax.dynamic_slice_in_dim(amp_tiles, first, group_size, 0)
        live_mask = (first + jnp.arange(group_size, dtype=jnp.int32) < live_count).astype(
            jnp.float32
        )
        return running + jnp.einsum(
            "kpw,kaw->pa",
            amp_block,
            int_block * live_mask[:, None, None],
            precision=lax.Precision.HIGHEST,
        )

    rounds = (live_count + group_size - 1) // group_size
    return lax.fori_loop(
        jnp.int32(0), rounds, step, jnp.zeros((pair_count, int_tiles.shape[1]), jnp.float32)
    )


def body(amplitude, integrals, task_count, task_owner, task_local):
    vir_size = lax.axis_size("vir")
    slot_count = integrals.shape[2]
    tile_width = integrals.shape[4]
    pair_rows = lax.all_gather(amplitude, "occ", axis=0, tiled=True)
    pair_count = pair_rows.shape[0]
    per_device = pair_rows.shape[1] // tile_width
    tile_view = pair_rows.reshape(pair_count, per_device, tile_width)
    owners = task_owner[0, 0, :, 0]
    tile_local = task_local[0, 0]
    int_tiles = integrals[0, 0]
    own_count = task_count[0, 0]
    capacity = max(2, -(-slot_count // vir_size))
    positions = jnp.arange(slot_count, dtype=jnp.int32)
    earlier = (owners[None, :] == owners[:, None]) & (positions[None, :] < positions[:, None])
    rank_among = jnp.sum(earlier.astype(jnp.int32), axis=1)
    target = owners * capacity + rank_among
    requests = jnp.zeros((vir_size * capacity,), jnp.int32).at[target].set(tile_local)
    requests = requests.reshape(vir_size, capacity)
    picked = jnp.take(
        tile_view, lax.all_to_all(requests, "vir", split_axis=0, concat_axis=0, tiled=True), axis=1
    )
    picked = jnp.transpose(picked, (1, 2, 0, 3))
    replies = lax.all_to_all(picked, "vir", split_axis=0, concat_axis=0, tiled=True)
    fetched = replies.reshape(vir_size * capacity, pair_count, tile_width)[target]
    partial_sum = accumulate(int_tiles, fetched, own_count)
    return lax.psum_scatter(partial_sum, "occ", scatter_dimension=0, tiled=True)


def solution(mesh):
    in_specs = (
        P("occ", "vir"),
        P("occ", "vir", None, None, None),
        P("occ", "vir"),
        P("occ", "vir", None, None),
        P("occ", "vir", None),
    )
    out_specs = P("occ", "vir")
    return jax.shard_map(body, mesh=mesh, in_specs=in_specs, out_specs=out_specs, check_vma=False)
```

profile of v0, /device:TPU:1, one launch (start us, length us, event | category | flops | bytes accessed | tf_op | source)
XLA Modules:
  0.0 504.9 jit_solution(13783275522461723040)
XLA Ops:
  6.5 0.0 all-gather.2.cloned.1.call-start
  6.5 0.7 all-gather.2.cloned.1.call-update
  7.3 0.9 convert_reduce_fusion
  8.2 0.7 fusion.7
  8.8 0.9 scatter_custom_fusion
  9.7 0.1 all_to_all.13
  9.9 32.2 %all_to_all.20 = s32[64,1,2]{2,1,0:T(1,128)S(1)} all-to-all(s32[64,1,2]{2,1,0:T(1,128)S(1)} %bitcast.32), channel_id=1, replica_groups=mesh['occ'=8,'vir'=64] {'vir'}, dimensions={0} | all-to-all | bytes 1024 | tf_op jit(solution)/shard_map/all_to_all | solution.py:54
  42.1 0.1 copy.27
  42.2 0.1 copy.31
  42.3 0.1 reshape.84
  42.4 0.1 copy.28
  42.5 4.0 all-gather.2.cloned.1.call-done
  46.6 1.6 copy.29
  48.2 0.4 copy.32
  48.6 4.3 gather_fusion
  52.9 7.2 %broadcast_select_fusion = f32[64,2,128,128]{3,2,1,0:T(8,128)} fusion(f32[64,2,128,128]{3,2,1,0:T(8,128)} %bitcast.29, pred[64,2]{1,0:T(8,128)(4,1)S(1)} %copy.28), kind=kLoop, calls=%fused_computation.11 | loop fusion | flops 2097152 | bytes 16777344 | tf_op jit(solution)/shard_map/jit(_take)/select_n | solution.py:53
  60.1 15.6 %all-to-all-start.1 = ((f32[64,2,128,128]{3,2,1,0:T(8,128)}), f32[64,2,128,128]{3,2,1,0:T(8,128)}, u32[]{:S(2)}, u32[]{:S(2)}) async-start(f32[64,2,128,128]{3,2,1,0:T(8,128)} %broadcast_select_fusion), calls=%async_computation.1 | async-start | bytes 16777216 | tf_op jit(solution)/shard_map/all_to_all | solution.py:57
  75.7 0.0 reduce-scatter.2.cloned.1.call-start
  76.4 364.9 %all-to-all-done.1 = f32[64,2,128,128]{3,2,1,0:T(8,128)} async-done(((f32[64,2,128,128]{3,2,1,0:T(8,128)}), f32[64,2,128,128]{3,2,1,0:T(8,128)}, u32[]{:S(2)}, u32[]{:S(2)}) %all-to-all-start.1) | async-done | bytes 8388640 | tf_op jit(solution)/shard_map/all_to_all | solution.py:57
  441.3 6.2 %gather_fusion.1 = f32[64,128,128]{2,1,0:T(8,128)} fusion(f32[128,128,128]{2,1,0:T(8,128)} %bitcast.12, s32[1024]{0:T(1024)S(1)} %pad_clamp_fusion), kind=kCustom, calls=%fused_computation.1 | custom fusion | bytes 8388864 | tf_op jit(solution)/shard_map/gather | solution.py:58
  447.5 7.2 %while.10 = (s32[]{:T(128)}, f32[128,32]{0,1:T(8,128)S(1)}, s32[]{:T(128)}, f32[64,128,128]{2,1,0:T(8,128)}, f32[64,32,128]{2,1,0:T(8,128)}, /*index=5*/s32[]{:T(128)}, s32[]{:T(128)}, s32[]{:T(128)}, s32[]{:T(128)}, s32[]{:T(128)}) while((s32[]{:T(128)}, f32[128,32]{0,1:T(8,128)S(1)}, s32[]{:T(128)}, f32[64,128,128]{2,1,0:T(8,128)}, ...), condition=%wide.region_3.4_spmd, body=%wide.region_2.3_spmd.sunk | while | flops 50368540 | bytes 689371 | solution.py:29
  447.5 0.6 compare_convert_fusion.2
  448.1 1.7 fusion.15
  449.9 0.7 compare_convert_fusion.2
  450.6 1.7 fusion.15
  452.3 0.7 compare_convert_fusion.2
  453.0 1.7 fusion.15
  454.7 0.7 copy.33
  455.4 0.0 reduce-scatter.2.cloned.1.call-update
  455.4 42.6 %reduce-scatter.2.cloned.1.call-done = f32[16,32]{1,0:T(8,128)} async-done(((f32[128,32]{1,0:T(8,128)}), f32[16,32]{1,0:T(8,128)}) %reduce-scatter.2.cloned.1.call-update) | async-done | bytes 2064 | tf_op jit(solution)/shard_map/reduce_scatter | solution.py:60
  (5 shorter events, 0.0 us)
Async XLA Ops:
  6.5 40.0 %all-gather.2.cloned.1.call-start = ((), (), s32[]{:S(2)}) async-start(), calls=%async_computation.3 | async-start | bytes 1327104 | tf_op jit(solution)/shard_map/all_gather | solution.py:38
  60.1 381.2 %all-to-all-start.1 = ((f32[64,2,128,128]{3,2,1,0:T(8,128)}), f32[64,2,128,128]{3,2,1,0:T(8,128)}, u32[]{:S(2)}, u32[]{:S(2)}) async-start(f32[64,2,128,128]{3,2,1,0:T(8,128)} %broadcast_select_fusion), calls=%async_computation.1 | async-start | bytes 16777216 | tf_op jit(solution)/shard_map/all_to_all | solution.py:57
  75.7 422.4 %reduce-scatter.2.cloned.1.call-start = ((), (), s32[]{:S(2)}) async-start(), calls=%async_computation.4 | async-start | bytes 73728 | tf_op jit(solution)/shard_map/reduce_scatter | solution.py:60
Sparse Core Ops, SparseCore 0:
  9.5 37.0 all-gather.1
  455.6 42.4 reduce-scatter.1
where the time goes:
time: 506 us; the launch traced here: 505 us
  waiting for transfers between devices  412 us (81%)
  blocking collectives  32.2 us (6%)
  starting transfers between devices  15.6 us (3%)
  local copies, waits for them, and re-layouts  14.6 us (3%)
  between operations  14.1 us (3%)
  other arithmetic  10.8 us (2%)
  matrix products  5.17 us (1%)
    all_to_all x1, waiting for transfers between devices, body(): lax.all_to_all(picked, 'vir', split_axis=0, concat_axis=0, tiled=True)  365 us
    reduce_scatter x1, waiting for transfers between devices, body(): return lax.psum_scatter(partial_sum, 'occ', scatter_dimension=0, tiled=True)  42.6 us
    all_to_all x1, blocking collectives, body(): lax.all_to_all(requests, 'vir', split_axis=0, concat_axis=0, tiled=True)  32.2 us
    all_to_all x1, starting transfers between devices, body(): lax.all_to_all(picked, 'vir', split_axis=0, concat_axis=0, tiled=True)  15.6 us
  transfers between devices with their start and end apart: 3, of which 3 were waited for; matrix products, arithmetic and copies ran while one was open for 1% of the time, Pallas kernels for 0%

commit v1 on v0

v1 whole, which is shorter than its diff:
```python
import functools

import jax
import jax.numpy as jnp
from jax import lax
from jax.experimental import pallas as pl
from jax.experimental.pallas import tpu as pltpu
from jax.sharding import PartitionSpec as P

MESH = pl.DeviceIdType.MESH

NX, NY, NZ = 4, 4, 16
PAIRS = 16
TW = 128
TPD = 18
A_TILES = 11
B_TILES = TPD - A_TILES
SLOTS = 64
AB = 32
N_OCC = 8
N_TILES = NX * NZ * TPD
CHUNKS = 4
CHUNK = SLOTS // CHUNKS
GROUP = 8
COPIES = 160


def kernel(amp, ints, ids, out, buf_a, buf_b, buf_i, buf_ids, ids_s, amp_hi, amp_lo, int_hi, int_lo, total,
           own_sem, send_sem, recv_sem):
    o, v = lax.axis_index("occ"), lax.axis_index("vir")
    y, c = o // 2, o % 2
    x, z = v // NZ, v % NZ

    def at(yy, cc, xx, zz):
        return (yy * 2 + cc, xx * NZ + zz)

    xr, xl, xo = (x + 1) % NX, (x + NX - 1) % NX, (x + 2) % NX
    yr, yl, yo = (y + 1) % NY, (y + NY - 1) % NY, (y + 2) % NY
    to_xr, to_xl = at(y, c, xr, z), at(y, c, xl, z)
    to_yr, to_yl = at(yr, c, x, z), at(yl, c, x, z)
    to_zr, to_zl = at(y, c, x, (z + 1) % NZ), at(y, c, x, (z + NZ - 1) % NZ)
    to_co = at(y, 1 - c, x, z)

    own = [
        pltpu.make_async_copy(amp.at[:, pl.ds(0, A_TILES * TW)], buf_a.at[z, x], own_sem.at[0]),
        pltpu.make_async_copy(amp.at[:, pl.ds(A_TILES * TW, B_TILES * TW)], buf_b.at[z, x], own_sem.at[1]),
        pltpu.make_async_copy(ints, buf_i.at[o], own_sem.at[2]),
        pltpu.make_async_copy(ids, buf_ids.at[o], own_sem.at[3]),
    ]
    for copy in own:
        copy.start()

    barrier = pltpu.get_barrier_semaphore()
    for device in (to_xr, to_xl, to_yr, to_yl, to_zr, to_zl, to_co):
        pl.semaphore_signal(barrier, inc=1, device_id=device, device_id_type=MESH)
    pl.semaphore_wait(barrier, 7)

    copies = []

    def send(ref, device):
        n = len(copies)
        copy = pltpu.make_async_remote_copy(
            src_ref=ref, dst_ref=ref, send_sem=send_sem.at[n], recv_sem=recv_sem.at[n],
            device_id=device, device_id_type=MESH,
        )
        copy.start()
        copies.append(copy)
        return copy

    def split(value):
        hi = value.astype(jnp.bfloat16)
        return hi, (value - hi.astype(jnp.float32)).astype(jnp.bfloat16)

    def convert_tiles(buf, zb, xb, first, count):
        def one(t, carry):
            value = buf[zb, xb, :, pl.ds(pl.multiple_of(t * TW, TW), TW)]
            hi, lo = split(value)
            tile = (xb * NZ + zb) * TPD + first + t
            amp_hi[tile] = hi
            amp_lo[tile] = lo
            return carry

        lax.fori_loop(0, count, one, 0)

    def convert_a(zb, xb):
        convert_tiles(buf_a, zb, xb, 0, A_TILES)

    def convert_b(zb):
        def one(xb, carry):
            convert_tiles(buf_b, zb, xb, A_TILES, B_TILES)
            return carry

        lax.fori_loop(0, NX, one, 0)

    def convert_ints(oo, q):
        def one(t, carry):
            hi, lo = split(buf_i[oo, q * CHUNK + t])
            int_hi[oo * SLOTS + q * CHUNK + t] = hi
            int_lo[oo * SLOTS + q * CHUNK + t] = lo
            return carry

        lax.fori_loop(0, CHUNK, one, 0)

    top, bottom = pl.ds(0, PAIRS // 2), pl.ds(PAIRS // 2, PAIRS // 2)

    order = [z]
    for s in range(1, NZ // 2):
        order += [(z + NZ - s) % NZ, (z + s) % NZ]
    order.append((z + NZ // 2) % NZ)
    ring_a = {}

    def a_send(s):
        if s == 0:
            right, left = buf_a.at[z, x], buf_a.at[z, x]
        else:
            right, left = buf_a.at[order[2 * s - 1], x], buf_a.at[order[2 * s], x]
        if s == NZ // 2 - 1:
            right = buf_a.at[order[2 * s - 1], x, top]
            left = buf_a.at[order[2 * s], x, bottom]
        ring_a[s] = send(right, to_zr), send(left, to_zl)

    def a_step(s):
        for copy in ring_a[s]:
            copy.wait_recv()
        if s < NZ // 2 - 1:
            a_send(s + 1)

    full_x, half_x = {}, {}

    def x_issue(i):
        block = buf_a.at[order[i], x]
        full_x[i] = send(block, to_xr), send(block, to_xl)

    def x_forward(i):
        full_x[i][0].wait_recv()
        right = send(buf_a.at[order[i], xl, top], to_xr)
        full_x[i][1].wait_recv()
        half_x[i] = right, send(buf_a.at[order[i], xr, bottom], to_xl)
        for xb in (x, xl, xr):
            convert_a(order[i], xb)

    def x_finish(i):
        for copy in half_x[i]:
            copy.wait_recv()
        convert_a(order[i], xo)

    state_b = {}

    def b_issue():
        state_b["full"] = send(buf_b.at[z, x], to_xr), send(buf_b.at[z, x], to_xl)

    def b_forward():
        state_b["full"][0].wait_recv()
        right = send(buf_b.at[z, xl, top], to_xr)
        state_b["full"][1].wait_recv()
        state_b["half"] = right, send(buf_b.at[z, xr, bottom], to_xl)

    def b_finish():
        for copy in state_b["half"]:
            copy.wait_recv()
        b_send(0)
        convert_b(z)

    ring_b = {}

    def b_send(s):
        if s == 0:
            right, left = z, z
        else:
            right, left = order[2 * s - 1], order[2 * s]
        ring_b[s] = []
        for first in (0, 2):
            if s == NZ // 2 - 1:
                ring_b[s] += [send(buf_b.at[right, pl.ds(first, 1)], to_zr), send(buf_b.at[left, pl.ds(first + 1, 1)], to_zl)]
            else:
                ring_b[s] += [send(buf_b.at[right, pl.ds(first, 2)], to_zr), send(buf_b.at[left, pl.ds(first, 2)], to_zl)]

    def b_step(s):
        for copy in ring_b[s]:
            copy.wait_recv()
        if s < NZ // 2 - 1:
            b_send(s + 1)
            convert_b(order[2 * s + 1])
            convert_b(order[2 * s + 2])
        else:
            convert_b(order[NZ - 1])

    def line(yy, cc):
        return yy * 2 + cc

    full_i, half_i, core_i = {}, {}, {}

    def piece(oo, first, count):
        return buf_i.at[oo, pl.ds(first, count)]

    def i_issue(q):
        block = piece(o, q * CHUNK, CHUNK)
        full_i[q] = send(block, to_yr), send(block, to_yl)
        core_i[q] = [send(block, to_co)]

    def i_forward(q):
        full_i[q][0].wait_recv()
        right = send(piece(line(yl, c), q * CHUNK, CHUNK // 2), to_yr)
        core_i[q].append(send(piece(line(yl, c), q * CHUNK, CHUNK), to_co))
        full_i[q][1].wait_recv()
        half_i[q] = right, send(piece(line(yr, c), q * CHUNK + CHUNK // 2, CHUNK // 2), to_yl)
        core_i[q].append(send(piece(line(yr, c), q * CHUNK, CHUNK), to_co))
        for yy in (y, yl, yr):
            convert_ints(line(yy, c), q)

    def i_finish(q):
        for copy in half_i[q]:
            copy.wait_recv()
        core_i[q].append(send(piece(line(yo, c), q * CHUNK, CHUNK), to_co))
        convert_ints(line(yo, c), q)

    def i_core(q):
        for copy in core_i[q]:
            copy.wait_recv()
        for yy in range(NY):
            convert_ints(line(yy, 1 - c), q)

    def ids_issue():
        block = buf_ids.at[o]
        return [send(block, to_yr), send(block, to_yl), send(block, to_co)]

    def ids_forward(sent):
        sent[0].wait_recv()
        sent[1].wait_recv()
        return [
            send(buf_ids.at[line(yl, c)], to_yr),
            send(buf_ids.at[line(yl, c)], to_co),
            send(buf_ids.at[line(yr, c)], to_co),
        ]

    for copy in own:
        copy.wait()
    a_send(0)
    b_issue()
    x_issue(0)
    ids_sent = ids_issue()
    for q in range(CHUNKS):
        i_issue(q)
    amp_hi[N_TILES] = jnp.zeros((PAIRS, TW), jnp.bfloat16)
    amp_lo[N_TILES] = jnp.zeros((PAIRS, TW), jnp.bfloat16)
    total[...] = jnp.zeros_like(total)

    a_at = {0: 0, 2: 1, 3: 2, 5: 3, 6: 4, 8: 5, 9: 6, 11: 7}
    b_at = {4: 0, 7: 1, 10: 2, 12: 3, 13: 4, 15: 5, 16: 6, 17: 7}
    i_at = {3: 0, 5: 1, 7: 2, 9: 3}
    f_at = {6: 0, 8: 1, 10: 2, 12: 3}
    k_at = {9: 0, 11: 1, 13: 2, 15: 3}
    ids_all = []
    for it in range(18):
        if it in a_at:
            a_step(a_at[it])
        if it == 0:
            b_forward()
        if 1 <= it < 16:
            x_issue(it)
        if it == 1:
            b_finish()
            ids_all = ids_forward(ids_sent)
        if 1 <= it < 17:
            x_forward(it - 1)
        if 2 <= it:
            x_finish(it - 2)
        if it == 2:
            ids_all[0].wait_recv()
            ids_all.append(send(buf_ids.at[line(yo, c)], to_co))
        if it in b_at:
            b_step(b_at[it])
        if it in i_at:
            i_forward(i_at[it])
        if it in f_at:
            i_finish(f_at[it])
        if it in k_at:
            i_core(k_at[it])
        if it == 8:
            for copy in [ids_sent[2]] + ids_all[1:]:
                copy.wait_recv()
            load = pltpu.make_async_copy(buf_ids, ids_s, own_sem.at[4])
            load.start()
            load.wait()

    def tiles(ref, g):
        oo, first = g // (SLOTS // GROUP), (g % (SLOTS // GROUP)) * GROUP
        return jnp.concatenate([ref[ids_s[oo, 0, first + j]] for j in range(GROUP)], axis=0)

    def rows(ref, g):
        return ref[pl.ds(g * GROUP, GROUP)].reshape(GROUP * AB, TW)

    def dot(a, b):
        return lax.dot_general(a, b, (((1,), (1,)), ((), ())), preferred_element_type=jnp.float32)

    def product(h, carry):
        g = 2 * h
        a_hi = jnp.concatenate([tiles(amp_hi, g), tiles(amp_hi, g + 1)], axis=1)
        a_lo = jnp.concatenate([tiles(amp_lo, g), tiles(amp_lo, g + 1)], axis=1)
        b_hi = jnp.concatenate([rows(int_hi, g), rows(int_hi, g + 1)], axis=1)
        b_lo = jnp.concatenate([rows(int_lo, g), rows(int_lo, g + 1)], axis=1)
        total[...] += dot(a_hi, b_hi) + dot(a_lo, b_hi) + dot(a_hi, b_lo)
        return carry

    lax.fori_loop(0, N_OCC * SLOTS // GROUP // 2, product, 0)
    result = total[pl.ds(0, PAIRS), pl.ds(0, AB)]
    for j in range(1, GROUP):
        result = result + total[pl.ds(j * PAIRS, PAIRS), pl.ds(j * AB, AB)]
    out[...] = result
    for copy in copies:
        copy.wait_send()


def body(amplitude, integrals, task_count, task_owner, task_local):
    live = jnp.arange(SLOTS, dtype=jnp.int32) < task_count[0, 0]
    ids = jnp.where(live, task_owner[0, 0, :, 0] * TPD + task_local[0, 0], N_TILES)
    ids = jnp.broadcast_to(jnp.pad(ids, (0, TW - SLOTS))[None, :], (8, TW))
    f32, bf16 = jnp.float32, jnp.bfloat16
    return pl.pallas_call(
        kernel,
        out_shape=jax.ShapeDtypeStruct((PAIRS, AB), f32),
        in_specs=[pl.BlockSpec(memory_space=pl.ANY)] * 3,
        out_specs=pl.BlockSpec(memory_space=pltpu.VMEM),
        scratch_shapes=[
            pltpu.VMEM((NZ, NX, PAIRS, A_TILES * TW), f32),
            pltpu.VMEM((NZ, NX, PAIRS, B_TILES * TW), f32),
            pltpu.VMEM((N_OCC, SLOTS, AB, TW), f32),
            pltpu.VMEM((N_OCC, 8, TW), jnp.int32),
            pltpu.SMEM((N_OCC, 8, TW), jnp.int32),
            pltpu.VMEM((N_TILES + 1, PAIRS, TW), bf16),
            pltpu.VMEM((N_TILES + 1, PAIRS, TW), bf16),
            pltpu.VMEM((N_OCC * SLOTS, AB, TW), bf16),
            pltpu.VMEM((N_OCC * SLOTS, AB, TW), bf16),
            pltpu.VMEM((GROUP * PAIRS, GROUP * AB), f32),
            pltpu.SemaphoreType.DMA((5,)),
            pltpu.SemaphoreType.DMA((COPIES,)),
            pltpu.SemaphoreType.DMA((COPIES,)),
        ],
        compiler_params=pltpu.CompilerParams(
            collective_id=0, has_side_effects=True, vmem_limit_bytes=48 * 1024 * 1024
        ),
    )(amplitude, integrals[0, 0], ids)


def solution(mesh):
    in_specs = (
        P("occ", "vir"),
        P("occ", "vir", None, None, None),
        P("occ", "vir"),
        P("occ", "vir", None, None),
        P("occ", "vir", None),
    )
    return jax.shard_map(body, mesh=mesh, in_specs=in_specs, out_specs=P("occ", "vir"), check_vma=False)
```

time: 506 us -> 116 us (0.23)
  the two profiles are of different devices: /device:TPU:1 before, /device:TPU:34 now
where the time goes in v1:
time: 116 us
  Pallas kernels  111 us (96%)
  local copies, waits for them, and re-layouts  3.4 us (3%)
    pallas_call x1, Pallas kernels, body(): pl.pallas_call(kernel, out_shape=jax.ShapeDtypeStruct((PAIRS, AB), f32),...  111 us
    unnamed x9, local copies, waits for them, and re-layouts  3.38 us

profile of v1, /device:TPU:34, one launch (start us, length us, event | category | flops | bytes accessed | tf_op | source)
XLA Modules:
  0.0 115.6 jit_solution(12498227115844682801)
XLA Ops:
  0.7 0.0 copy-start.2
  0.7 0.0 copy-start.3
  0.7 0.6 copy-done.2
  1.3 0.0 copy-done.3
  1.3 0.0 copy-start
  1.4 1.2 %copy-done = f32[1,1,64,32,128]{4,3,2,1,0:T(8,128)S(1)} copy-done((f32[1,1,64,32,128]{4,3,2,1,0:T(8,128)S(1)}, f32[1,1,64,32,128]{4,3,2,1,0:T(8,128)}, u32[]{:S(2)}) %copy-start) | copy-done | bytes 1048600
  2.6 0.0 copy-start.1
  2.6 0.9 copy-done.1
  3.5 111.5 %shard_map.55 = f32[16,32]{1,0:T(8,128)S(1)} custom-call(f32[16,2304]{1,0:T(8,128)S(1)} %copy-done.1, f32[64,32,128]{2,1,0:T(8,128)S(1)} %bitcast.9, s32[8,128]{1,0:T(8,128)S(1)} %broadcast_in_dim.11.ids), custom_call_target="tpu_custom_call" | custom-call | tf_op jit(solution)/shard_map/pallas_call | solution.py:319
  115.0 0.6 copy.8
  (3 shorter events, 0.0 us)
Async XLA Ops:
  0.7 0.7 copy-start.2
  0.7 0.7 copy-start.3
  1.3 1.2 %copy-start = (f32[1,1,64,32,128]{4,3,2,1,0:T(8,128)S(1)}, f32[1,1,64,32,128]{4,3,2,1,0:T(8,128)}, u32[]{:S(2)}) copy-start(f32[1,1,64,32,128]{4,3,2,1,0:T(8,128)} %param.6) | copy-start | bytes 3145732
  2.6 0.9 copy-start.1

commit v2 on v0

v2 whole, which is shorter than its diff:
```python
import jax
import jax.numpy as jnp
from jax import lax
from jax.experimental import pallas as pl
from jax.experimental.pallas import tpu as pltpu
from jax.sharding import PartitionSpec as P

MESH = pl.DeviceIdType.MESH

NX, NY, NZ = 4, 4, 16
PAIRS = 16
TW = 128
TPD = 18
SLOTS = 64
AB = 32
N_OCC = 8
N_TILES = NX * NZ * TPD
GROUP = 8
N_GROUPS = N_OCC * SLOTS // GROUP
DEPTH = 4

PARTS = 3
LAG = 5
TABLE = (
    (128, 64, 0, -1, -1, 65, 79, 15, 80, 16, 81, 14, 142, 2, 31, 77, 94, 67, 141, 18, 93, 76, 147, 157, 140, 68, 148, 4, 75, 11,
     69, 74, 149, 181, 27, 5, 90, 150, 137, 54, 70, 26, 102, 153, 25, 82, 138, 158, 95, -1),
    (64, 128, 0, -1, -1, 79, 176, 15, 129, 1, 66, 78, 14, 130, 2, 77, 67, 191, 62, 178, 68, 115, 140, 12, 61, 116, 51, 75, 188,
     60, 69, 74, 123, 187, 10, 53, 73, 186, 150, 54, 137, 72, 121, 136, 55, 151, 148, 141, 49, -1),
    (64, 0, 128, -1, -1, 65, 144, 129, 1, 16, 66, 145, 81, 2, 160, 67, 146, 130, 178, 50, 3, 147, 18, 179, 51, 68, 4, 148, 180,
     52, 100, 35, 149, 69, 53, 181, 101, 150, 70, 54, 182, 102, 166, 21, 55, 86, 103, 167, 22, -1),
    (64, 0, 128, -1, -1, 79, 15, 143, 144, 176, 78, 95, 142, 14, 191, 77, 30, 141, 13, 62, 125, 76, 29, 140, 12, 109, 75, 188,
     139, 11, 156, 74, 187, 138, 27, 10, 73, 90, 137, 26, 9, 58, 89, 153, 25, 8, 120, 60, 114, 41),
)
STEPS = len(TABLE[0])
PT = TPD // PARTS
STEP_OF = ((0, 0, 0), (1, 1, 0), (2, 0, 1), (3, 0, -1))

Y_TASKS = 4
Y_OWN = SLOTS // Y_TASKS
Y_MSGS = Y_OWN + Y_OWN // 2
Y_STEP = [m * (STEPS - 12) // Y_MSGS for m in range(Y_MSGS)]
BATCH = 4
COPIES = 4 * STEPS + 2 * Y_MSGS + 24


def kernel(amp, ints, count_hbm, owner_hbm, local_hbm, out, buf_a, buf_i, buf_ids, ids_s, count_s, owner_v, local_v,
           amp_hi, amp_lo, int_hi, int_lo, total, own_sem, send_sem, recv_sem):
    o, v = lax.axis_index("occ"), lax.axis_index("vir")
    y, c = o // 2, o % 2
    x, z = v // NZ, v % NZ

    def at(yy, cc, xx, zz):
        return (yy * 2 + cc, xx * NZ + zz)

    def line(yy, cc):
        return yy * 2 + cc

    yr, yl, yo = (y + 1) % NY, (y + NY - 1) % NY, (y + 2) % NY
    to_yr, to_yl = at(yr, c, x, z), at(yl, c, x, z)
    to_co = at(y, 1 - c, x, z)
    to = (
        at(y, c, (x + 1) % NX, z),
        at(y, c, (x + NX - 1) % NX, z),
        at(y, c, x, (z + 1) % NZ),
        at(y, c, x, (z + NZ - 1) % NZ),
    )

    own = [
        pltpu.make_async_copy(count_hbm, count_s, own_sem.at[0]),
        pltpu.make_async_copy(owner_hbm, owner_v, own_sem.at[1]),
        pltpu.make_async_copy(local_hbm, local_v, own_sem.at[2]),
        pltpu.make_async_copy(ints, buf_i.at[o], own_sem.at[3]),
    ]
    for p in range(PARTS):
        own.append(pltpu.make_async_copy(amp.at[:, pl.ds(p * PT * TW, PT * TW)], buf_a.at[p, z, x], own_sem.at[4 + p]))
    for copy in own:
        copy.start()

    barrier = pltpu.get_barrier_semaphore()
    for device in (to_yr, to_yl, to_co) + to:
        pl.semaphore_signal(barrier, inc=1, device_id=device, device_id_type=MESH)

    copies = []

    def send(ref, device):
        n = len(copies)
        copy = pltpu.make_async_remote_copy(
            src_ref=ref, dst_ref=ref, send_sem=send_sem.at[n], recv_sem=recv_sem.at[n],
            device_id=device, device_id_type=MESH,
        )
        copy.start()
        copies.append(copy)
        return copy

    def split(value):
        hi = value.astype(jnp.bfloat16)
        return hi, (value - hi.astype(jnp.float32)).astype(jnp.bfloat16)

    def place(code):
        p, dx, dz = code // 64, code // NZ % NX, code % NZ
        return p, (z + NZ - dz) % NZ, (x + NX - dx) % NX

    def convert_part(p, zb, xb):
        first = (xb * NZ + zb) * TPD + p * PT

        def one(t, carry):
            hi, lo = split(buf_a[p, zb, xb, :, pl.ds(pl.multiple_of(t * TW, TW), TW)])
            amp_hi[first + t] = hi
            amp_lo[first + t] = lo
            return carry

        lax.fori_loop(0, PT, one, 0)

    def convert_groups(oo, first, number):
        def one(j, carry):
            rows = buf_i[oo, pl.ds((first + j) * GROUP, GROUP)].reshape(GROUP * AB, TW)
            hi, lo = split(rows.T)
            g = oo * (SLOTS // GROUP) + first + j
            int_hi[g] = hi
            int_lo[g] = lo
            return carry

        lax.fori_loop(0, number, one, 0)

    def tasks(oo, m, number):
        return buf_i.at[oo, pl.ds(m * Y_TASKS, number * Y_TASKS)]

    for copy in own[:3]:
        copy.wait()
    slot = lax.broadcasted_iota(jnp.int32, (1, SLOTS), 1)
    ids = jnp.where(slot < count_s[0, 0], owner_v[...] * TPD + local_v[...], N_TILES)
    buf_ids[o] = jnp.zeros((8, TW), jnp.int32)
    buf_ids[o, :, pl.ds(0, SLOTS)] = jnp.broadcast_to(ids, (8, SLOTS))
    for copy in own[3:]:
        copy.wait()
    pl.semaphore_wait(barrier, 7)

    sent, sent_y, sent_co, sent_ids = {}, {}, [], []
    todo = {}

    def later(t, work):
        todo.setdefault(t, []).append(work)

    def to_core(t, oo, m, number):
        copy = send(tasks(oo, m, number), to_co)
        other = oo + 1 - 2 * c

        def work():
            copy.wait_recv()
            convert_groups(other, m * Y_TASKS // GROUP, number * Y_TASKS // GROUP)

        later(t + LAG, work)

    def y_arrived(t, m):
        for copy in sent_y[m]:
            copy.wait_recv()
        end = m + 1
        if end % BATCH:
            return
        first = end - BATCH
        groups = BATCH * Y_TASKS // GROUP
        if m < Y_OWN:
            for yy in (yl, yr):
                to_core(t, line(yy, c), first, BATCH)
                convert_groups(line(yy, c), first * Y_TASKS // GROUP, groups)
        else:
            for half in (0, Y_OWN // 2):
                to_core(t, line(yo, c), half + first - Y_OWN, BATCH)
                convert_groups(line(yo, c), (half + first - Y_OWN) * Y_TASKS // GROUP, groups)

    def y_send(m):
        if m < Y_OWN:
            block = tasks(o, m, 1)
            sent_y[m] = send(block, to_yr), send(block, to_yl)
        else:
            k = m - Y_OWN
            sent_y[m] = send(tasks(line(yl, c), k, 1), to_yr), send(tasks(line(yr, c), Y_OWN // 2 + k, 1), to_yl)

    for t in range(STEPS + 3 * LAG):
        if LAG <= t < STEPS + LAG:
            for copy in sent[t - LAG].values():
                copy.wait_recv()
        if t < STEPS:
            sent[t] = {}
            for d in range(4):
                if TABLE[d][t] >= 0:
                    p, zb, xb = place(TABLE[d][t])
                    sent[t][d] = send(buf_a.at[p, zb, xb], to[d])
        for m in range(Y_MSGS):
            if Y_STEP[m] == t:
                y_send(m)
        if t == 0:
            block = buf_ids.at[o]
            sent_ids = [send(block, to_yr), send(block, to_yl), send(block, to_co)]
            amp_hi[N_TILES] = jnp.zeros((PAIRS, TW), jnp.bfloat16)
            amp_lo[N_TILES] = jnp.zeros((PAIRS, TW), jnp.bfloat16)
            total[...] = jnp.zeros_like(total)
            for p in range(PARTS):
                convert_part(p, z, x)
        if t == 1:
            for q in range(0, Y_OWN, BATCH):
                to_core(t, o, q, BATCH)
            convert_groups(o, 0, SLOTS // GROUP)
        if t == LAG:
            sent_ids[0].wait_recv()
            sent_ids[1].wait_recv()
            sent_ids += [
                send(buf_ids.at[line(yl, c)], to_yr),
                send(buf_ids.at[line(yl, c)], to_co),
                send(buf_ids.at[line(yr, c)], to_co),
            ]
        if t == 2 * LAG:
            sent_ids[3].wait_recv()
            sent_ids.append(send(buf_ids.at[line(yo, c)], to_co))
        if t == 3 * LAG:
            for copy in [sent_ids[2]] + sent_ids[4:]:
                copy.wait_recv()
            load = pltpu.make_async_copy(buf_ids, ids_s, own_sem.at[0])
            load.start()
            load.wait()
        for m in range(Y_MSGS):
            if Y_STEP[m] + LAG == t:
                y_arrived(t, m)
        for work in todo.pop(t, []):
            work()
        if LAG <= t < STEPS + LAG:
            for d, dx, dz in STEP_OF:
                if TABLE[d][t - LAG] >= 0:
                    p, zb, xb = place(TABLE[d][t - LAG])
                    if d == 0:
                        xb = (xb + NX - 1) % NX
                    elif d == 1:
                        xb = (xb + 1) % NX
                    elif d == 2:
                        zb = (zb + NZ - 1) % NZ
                    else:
                        zb = (zb + 1) % NZ
                    convert_part(p, zb, xb)

    def tiles(ref, g):
        oo, first = g // (SLOTS // GROUP), (g % (SLOTS // GROUP)) * GROUP
        return jnp.concatenate([ref[ids_s[oo, 0, first + j]] for j in range(GROUP)], axis=0)

    def dot(a, b):
        return lax.dot_general(a, b, (((1,), (0,)), ((), ())), preferred_element_type=jnp.float32)

    def product(h, carry):
        g = DEPTH * h
        a_hi = jnp.concatenate([tiles(amp_hi, g + j) for j in range(DEPTH)], axis=1)
        a_lo = jnp.concatenate([tiles(amp_lo, g + j) for j in range(DEPTH)], axis=1)
        b_hi = int_hi[pl.ds(g, DEPTH)].reshape(DEPTH * TW, GROUP * AB)
        b_lo = int_lo[pl.ds(g, DEPTH)].reshape(DEPTH * TW, GROUP * AB)
        total[...] += dot(a_hi, b_hi) + dot(a_lo, b_hi) + dot(a_hi, b_lo)
        return carry

    lax.fori_loop(0, N_GROUPS // DEPTH, product, 0)
    result = total[pl.ds(0, PAIRS), pl.ds(0, AB)]
    for j in range(1, GROUP):
        result = result + total[pl.ds(j * PAIRS, PAIRS), pl.ds(j * AB, AB)]
    out[...] = result
    for copy in copies:
        copy.wait_send()


def body(amplitude, integrals, task_count, task_owner, task_local):
    f32, bf16 = jnp.float32, jnp.bfloat16
    return pl.pallas_call(
        kernel,
        out_shape=jax.ShapeDtypeStruct((PAIRS, AB), f32),
        in_specs=[pl.BlockSpec(memory_space=pltpu.HBM)] * 5,
        out_specs=pl.BlockSpec(memory_space=pltpu.VMEM),
        scratch_shapes=[
            pltpu.VMEM((PARTS, NZ, NX, PAIRS, PT * TW), f32),
            pltpu.VMEM((N_OCC, SLOTS, AB, TW), f32),
            pltpu.VMEM((N_OCC, 8, TW), jnp.int32),
            pltpu.SMEM((N_OCC, 8, TW), jnp.int32),
            pltpu.SMEM((1, 1), jnp.int32),
            pltpu.VMEM((1, SLOTS), jnp.int32),
            pltpu.VMEM((1, SLOTS), jnp.int32),
            pltpu.VMEM((N_TILES + 1, PAIRS, TW), bf16),
            pltpu.VMEM((N_TILES + 1, PAIRS, TW), bf16),
            pltpu.VMEM((N_GROUPS, TW, GROUP * AB), bf16),
            pltpu.VMEM((N_GROUPS, TW, GROUP * AB), bf16),
            pltpu.VMEM((GROUP * PAIRS, GROUP * AB), f32),
            pltpu.SemaphoreType.DMA((4 + PARTS,)),
            pltpu.SemaphoreType.DMA((COPIES,)),
            pltpu.SemaphoreType.DMA((COPIES,)),
        ],
        compiler_params=pltpu.CompilerParams(
            collective_id=0, has_side_effects=True, vmem_limit_bytes=64 * 1024 * 1024
        ),
    )(
        amplitude,
        integrals[0, 0],
        task_count,
        task_owner.reshape(1, SLOTS),
        task_local.reshape(1, SLOTS),
    )


def solution(mesh):
    in_specs = (
        P("occ", "vir"),
        P("occ", "vir", None, None, None),
        P("occ", "vir"),
        P("occ", "vir", None, None),
        P("occ", "vir", None),
    )
    return jax.shard_map(body, mesh=mesh, in_specs=in_specs, out_specs=P("occ", "vir"), check_vma=False)
```

time: 506 us -> 78.1 us (0.15)
  waiting for transfers between devices: 412 us -> 0 us
  Pallas kernels: 0 us -> 75.7 us
  blocking collectives: 32.2 us -> 0 us
  starting transfers between devices: 15.6 us -> 0 us
  between operations: 14.1 us -> 0.66 us
  local copies, waits for them, and re-layouts: 14.6 us -> 1.3 us
  other arithmetic: 10.8 us -> 0 us
  matrix products: 5.17 us -> 0 us
    all_to_all x1 -> x0, waiting for transfers between devices: 365 us -> none  [body(): lax.all_to_all(picked, 'vir', split_axis=0, concat_axis=0, tiled=True)]
    pallas_call x0 -> x1, Pallas kernels: none -> 75.7 us  [body(): pl.pallas_call(kernel, out_shape=jax.ShapeDtypeStruct((PAIRS, AB), f32),...]
    reduce_scatter x1 -> x0, waiting for transfers between devices: 42.6 us -> none  [body(): return lax.psum_scatter(partial_sum, 'occ', scatter_dimension=0, tiled=True)]
    all_to_all x1 -> x0, blocking collectives: 32.2 us -> none  [body(): lax.all_to_all(requests, 'vir', split_axis=0, concat_axis=0, tiled=True)]
    all_to_all x1 -> x0, starting transfers between devices: 15.6 us -> none  [body(): lax.all_to_all(picked, 'vir', split_axis=0, concat_axis=0, tiled=True)]
    gather x2 -> x0, local copies, waits for them, and re-layouts: 10.4 us -> none  [the longest x1 6.15 us: body(): replies.reshape(vir_size * capacity, pair_count, tile_width)[target]]
    select_n x3 -> x0, other arithmetic: 7.9 us -> none  [the longest x2 7.23 us: body(): jnp.take(tile_view, lax.all_to_all(requests, 'vir', split_axis=0, concat_...]
    dot_general x3 -> x0, matrix products: 5.17 us -> none  [step(): jnp.einsum('kpw,kaw->pa', amp_block, int_block * live_mask[:, None, None]...]
  transfers between devices with their start and end apart: 3 -> 0, of which waited for: 3 -> 0; matrix products, arithmetic and copies ran while one was open for 1% -> 0% of each run, Pallas kernels for 0% -> 0%
where the time goes in v2:
time: 78.1 us; the launch traced here: 77.6 us
  Pallas kernels  75.7 us (97%)
  local copies, waits for them, and re-layouts  1.3 us (2%)
    pallas_call x1, Pallas kernels, body(): pl.pallas_call(kernel, out_shape=jax.ShapeDtypeStruct((PAIRS, AB), f32),...  75.7 us

profile of v2, /device:TPU:1, one launch (start us, length us, event | category | flops | bytes accessed | tf_op | source)
XLA Modules:
  0.0 77.6 jit_solution(2385921582171084710)
XLA Ops:
  0.7 75.7 %shard_map.55 = f32[16,32]{1,0:T(8,128)} custom-call(f32[16,2304]{1,0:T(8,128)} %amp.1, f32[64,32,128]{2,1,0:T(8,128)} %bitcast.3, s32[1,1]{1,0:T(1,128)S(6)} %copy.7.count_hbm, s32[1,64]{1,0:T(1,128)} %bitcast.4, s32[1,64]{1,0:T(1,128)} %bitcast.5), custom_call_target="tpu_custom_call" | custom-call | tf_op jit(solution)/shard_map/pallas_call | solution.py:267
  76.3 1.3 %copy.8 = f32[16,32]{1,0:T(8,128)} copy(f32[16,32]{1,0:T(8,128)} %shard_map.55) | data formatting | bytes 4096

commit v3 on v2

--- a/solution.py
+++ b/solution.py
@@ -17,34 +17,41 @@
 N_TILES = NX * NZ * TPD
 GROUP = 8
 N_GROUPS = N_OCC * SLOTS // GROUP
-DEPTH = 4
+DEPTH = 16
 
 PARTS = 3
-LAG = 5
+LAGS = (3, 3, 3, 4, 4, 4, 5,)
+LAG = LAGS[-1]
 TABLE = (
-    (128, 64, 0, -1, -1, 65, 79, 15, 80, 16, 81, 14, 142, 2, 31, 77, 94, 67, 141, 18, 93, 76, 147, 157, 140, 68, 148, 4, 75, 11,
-     69, 74, 149, 181, 27, 5, 90, 150, 137, 54, 70, 26, 102, 153, 25, 82, 138, 158, 95, -1),
-    (64, 128, 0, -1, -1, 79, 176, 15, 129, 1, 66, 78, 14, 130, 2, 77, 67, 191, 62, 178, 68, 115, 140, 12, 61, 116, 51, 75, 188,
-     60, 69, 74, 123, 187, 10, 53, 73, 186, 150, 54, 137, 72, 121, 136, 55, 151, 148, 141, 49, -1),
-    (64, 0, 128, -1, -1, 65, 144, 129, 1, 16, 66, 145, 81, 2, 160, 67, 146, 130, 178, 50, 3, 147, 18, 179, 51, 68, 4, 148, 180,
-     52, 100, 35, 149, 69, 53, 181, 101, 150, 70, 54, 182, 102, 166, 21, 55, 86, 103, 167, 22, -1),
-    (64, 0, 128, -1, -1, 79, 15, 143, 144, 176, 78, 95, 142, 14, 191, 77, 30, 141, 13, 62, 125, 76, 29, 140, 12, 109, 75, 188,
-     139, 11, 156, 74, 187, 138, 27, 10, 73, 90, 137, 26, 9, 58, 89, 153, 25, 8, 120, 60, 114, 41),
+    (128, 64, 0, 144, 1, 143, 65, 129, 15, 130, 159, 14, 77, 18, 146, 67, 131, 30, 13, 76, 19, 147, 12, 4, 29, 84, 140, 28, 5, 74,
+     139, 69, 20, 6, 134, 155, 21, 9, 7, 71, 135, 22, 25, 136, 23, 100, 31, -1),
+    (64, 128, 0, 79, 112, 1, 48, 15, 78, 130, 127, 49, 77, 14, 190, 113, 67, 125, 3, 114, 189, 13, 12, 4, 75, 124, 188, 69, 11,
+     74, 5, 181, 10, 117, 59, 122, 70, 58, 9, 121, 7, 185, 183, 186, 120, 180, 129, -1),
+    (64, 0, 128, 112, 65, 129, 1, 160, 17, 49, 66, 130, 2, 113, 178, 18, 67, 3, 131, 179, 83, 68, 4, 132, 147, 98, 180, 5, 133,
+     69, 148, 181, 6, 134, 70, 53, 182, 165, 135, 101, 71, 183, 118, 25, 102, 85, 81, -1),
+    (64, 0, 128, 79, 176, 80, 15, 78, 143, 191, 95, 159, 14, 142, 77, 190, 158, 13, 141, 76, 125, 189, 12, 140, 75, 92, 188, 11,
+     28, 74, 108, 187, 10, 139, 122, 90, 186, 155, 138, 121, 89, 9, 25, 154, 57, 111, 169, 41),
 )
 STEPS = len(TABLE[0])
 PT = TPD // PARTS
-STEP_OF = ((0, 0, 0), (1, 1, 0), (2, 0, 1), (3, 0, -1))
 
 Y_TASKS = 4
 Y_OWN = SLOTS // Y_TASKS
 Y_MSGS = Y_OWN + Y_OWN // 2
 Y_STEP = [m * (STEPS - 12) // Y_MSGS for m in range(Y_MSGS)]
 BATCH = 4
-COPIES = 4 * STEPS + 2 * Y_MSGS + 24
+SEND_AGAIN, RECV_AGAIN = 7, 13
+Y_SEND_AGAIN, Y_RECV_AGAIN = 6, 9
+SINGLES = 24
+
+
+def lag(t):
+    return LAGS[min(t, len(LAGS) - 1)]
 
 
 def kernel(amp, ints, count_hbm, owner_hbm, local_hbm, out, buf_a, buf_i, buf_ids, ids_s, count_s, owner_v, local_v,
-           amp_hi, amp_lo, int_hi, int_lo, total, own_sem, send_sem, recv_sem):
+           amp_hi, amp_lo, int_hi, int_lo, total, own_sem, send_sem, recv_sem,
+           y_send_sem, y_recv_sem, one_send_sem, one_recv_sem):
     o, v = lax.axis_index("occ"), lax.axis_index("vir")
     y, c = o // 2, o % 2
     x, z = v // NZ, v % NZ
@@ -80,17 +87,19 @@
     for device in (to_yr, to_yl, to_co) + to:
         pl.semaphore_signal(barrier, inc=1, device_id=device, device_id_type=MESH)
 
-    copies = []
-
-    def send(ref, device):
-        n = len(copies)
+    def start(ref, device, send_one, recv_one):
         copy = pltpu.make_async_remote_copy(
-            src_ref=ref, dst_ref=ref, send_sem=send_sem.at[n], recv_sem=recv_sem.at[n],
-            device_id=device, device_id_type=MESH,
+            src_ref=ref, dst_ref=ref, send_sem=send_one, recv_sem=recv_one, device_id=device, device_id_type=MESH
         )
         copy.start()
-        copies.append(copy)
         return copy
+
+    singles = []
+
+    def send(ref, device):
+        n = len(singles)
+        singles.append(start(ref, device, one_send_sem.at[n], one_recv_sem.at[n]))
+        return singles[n]
 
     def split(value):
         hi = value.astype(jnp.bfloat16)
@@ -169,23 +178,34 @@
                 convert_groups(line(yo, c), (half + first - Y_OWN) * Y_TASKS // GROUP, groups)
 
     def y_send(m):
+        if m >= Y_SEND_AGAIN:
+            for copy in sent_y[m - Y_SEND_AGAIN]:
+                copy.wait_send()
         if m < Y_OWN:
-            block = tasks(o, m, 1)
-            sent_y[m] = send(block, to_yr), send(block, to_yl)
+            right = left = tasks(o, m, 1)
         else:
-            k = m - Y_OWN
-            sent_y[m] = send(tasks(line(yl, c), k, 1), to_yr), send(tasks(line(yr, c), Y_OWN // 2 + k, 1), to_yl)
+            right = tasks(line(yl, c), m - Y_OWN, 1)
+            left = tasks(line(yr, c), Y_OWN // 2 + m - Y_OWN, 1)
+        sent_y[m] = [
+            start(ref, device, y_send_sem.at[d, m % Y_SEND_AGAIN], y_recv_sem.at[d, m % Y_RECV_AGAIN])
+            for d, (ref, device) in enumerate(((right, to_yr), (left, to_yl)))
+        ]
 
     for t in range(STEPS + 3 * LAG):
-        if LAG <= t < STEPS + LAG:
-            for copy in sent[t - LAG].values():
+        arrived = [s for s in range(STEPS) if s + lag(s) == t]
+        for s in arrived:
+            for copy in sent[s].values():
                 copy.wait_recv()
         if t < STEPS:
+            for copy in sent.get(t - SEND_AGAIN, {}).values():
+                copy.wait_send()
             sent[t] = {}
             for d in range(4):
                 if TABLE[d][t] >= 0:
                     p, zb, xb = place(TABLE[d][t])
-                    sent[t][d] = send(buf_a.at[p, zb, xb], to[d])
+                    sent[t][d] = start(
+                        buf_a.at[p, zb, xb], to[d], send_sem.at[d, t % SEND_AGAIN], recv_sem.at[d, t % RECV_AGAIN]
+                    )
         for m in range(Y_MSGS):
             if Y_STEP[m] == t:
                 y_send(m)
@@ -223,10 +243,10 @@
                 y_arrived(t, m)
         for work in todo.pop(t, []):
             work()
-        if LAG <= t < STEPS + LAG:
-            for d, dx, dz in STEP_OF:
-                if TABLE[d][t - LAG] >= 0:
-                    p, zb, xb = place(TABLE[d][t - LAG])
+        for s in arrived:
+            for d in range(4):
+                if TABLE[d][s] >= 0:
+                    p, zb, xb = place(TABLE[d][s])
                     if d == 0:
                         xb = (xb + NX - 1) % NX
                     elif d == 1:
@@ -258,7 +278,9 @@
     for j in range(1, GROUP):
         result = result + total[pl.ds(j * PAIRS, PAIRS), pl.ds(j * AB, AB)]
     out[...] = result
-    for copy in copies:
+    left = [copy for t in range(STEPS - SEND_AGAIN, STEPS) for copy in sent[t].values()]
+    left += [copy for m in range(Y_MSGS - Y_SEND_AGAIN, Y_MSGS) for copy in sent_y[m]]
+    for copy in left + singles:
         copy.wait_send()
 
 
@@ -283,8 +305,12 @@
             pltpu.VMEM((N_GROUPS, TW, GROUP * AB), bf16),
             pltpu.VMEM((GROUP * PAIRS, GROUP * AB), f32),
             pltpu.SemaphoreType.DMA((4 + PARTS,)),
-            pltpu.SemaphoreType.DMA((COPIES,)),
-            pltpu.SemaphoreType.DMA((COPIES,)),
+            pltpu.SemaphoreType.DMA((4, SEND_AGAIN)),
+            pltpu.SemaphoreType.DMA((4, RECV_AGAIN)),
+            pltpu.SemaphoreType.DMA((2, Y_SEND_AGAIN)),
+            pltpu.SemaphoreType.DMA((2, Y_RECV_AGAIN)),
+            pltpu.SemaphoreType.DMA((SINGLES,)),
+            pltpu.SemaphoreType.DMA((SINGLES,)),
         ],
         compiler_params=pltpu.CompilerParams(
             collective_id=0, has_side_effects=True, vmem_limit_bytes=64 * 1024 * 1024

time: 78.1 us -> 72.6 us (0.930)
  Pallas kernels: 75.7 us -> 70.5 us
    pallas_call x1, Pallas kernels: 75.7 us -> 70.5 us  [body(): pl.pallas_call(kernel, out_shape=jax.ShapeDtypeStruct((PAIRS, AB), f32),...]
where the time goes in v3:
time: 72.6 us; the launch traced here: 72.4 us
  Pallas kernels  70.5 us (97%)
  local copies, waits for them, and re-layouts  1.3 us (2%)
    pallas_call x1, Pallas kernels, body(): pl.pallas_call(kernel, out_shape=jax.ShapeDtypeStruct((PAIRS, AB), f32),...  70.5 us

profile of v3, /device:TPU:1, one launch (start us, length us, event | category | flops | bytes accessed | tf_op | source)
XLA Modules:
  0.0 72.4 jit_solution(17797811922404379832)
XLA Ops:
  0.7 70.5 %shard_map.55 = f32[16,32]{1,0:T(8,128)} custom-call(f32[16,2304]{1,0:T(8,128)} %amp.1, f32[64,32,128]{2,1,0:T(8,128)} %bitcast.3, s32[1,1]{1,0:T(1,128)S(6)} %copy.7.count_hbm, s32[1,64]{1,0:T(1,128)} %bitcast.4, s32[1,64]{1,0:T(1,128)} %bitcast.5), custom_call_target="tpu_custom_call" | custom-call | tf_op jit(solution)/shard_map/pallas_call | solution.py:289
  71.1 1.3 %copy.8 = f32[16,32]{1,0:T(8,128)} copy(f32[16,32]{1,0:T(8,128)} %shard_map.55) | data formatting | bytes 4096

commit v4 on v3

--- a/solution.py
+++ b/solution.py
@@ -17,7 +17,6 @@
 N_TILES = NX * NZ * TPD
 GROUP = 8
 N_GROUPS = N_OCC * SLOTS // GROUP
-DEPTH = 16
 
 PARTS = 3
 LAGS = (3, 3, 3, 4, 4, 4, 5,)
@@ -87,18 +86,18 @@
     for device in (to_yr, to_yl, to_co) + to:
         pl.semaphore_signal(barrier, inc=1, device_id=device, device_id_type=MESH)
 
-    def start(ref, device, send_one, recv_one):
+    def start(ref, device, send_one, recv_one, source=None):
         copy = pltpu.make_async_remote_copy(
-            src_ref=ref, dst_ref=ref, send_sem=send_one, recv_sem=recv_one, device_id=device, device_id_type=MESH
+            src_ref=ref if source is None else source, dst_ref=ref, send_sem=send_one, recv_sem=recv_one, device_id=device, device_id_type=MESH
         )
         copy.start()
         return copy
 
     singles = []
 
-    def send(ref, device):
+    def send(ref, device, source=None):
         n = len(singles)
-        singles.append(start(ref, device, one_send_sem.at[n], one_recv_sem.at[n]))
+        singles.append(start(ref, device, one_send_sem.at[n], one_recv_sem.at[n], source))
         return singles[n]
 
     def split(value):
@@ -134,15 +133,15 @@
     def tasks(oo, m, number):
         return buf_i.at[oo, pl.ds(m * Y_TASKS, number * Y_TASKS)]
 
-    for copy in own[:3]:
-        copy.wait()
-    slot = lax.broadcasted_iota(jnp.int32, (1, SLOTS), 1)
-    ids = jnp.where(slot < count_s[0, 0], owner_v[...] * TPD + local_v[...], N_TILES)
-    buf_ids[o] = jnp.zeros((8, TW), jnp.int32)
-    buf_ids[o, :, pl.ds(0, SLOTS)] = jnp.broadcast_to(ids, (8, SLOTS))
-    for copy in own[3:]:
-        copy.wait()
     pl.semaphore_wait(barrier, 7)
+
+    def number_tasks():
+        for copy in own[:3]:
+            copy.wait()
+        slot = lax.broadcasted_iota(jnp.int32, (1, SLOTS), 1)
+        ids = jnp.where(slot < count_s[0, 0], owner_v[...] * TPD + local_v[...], N_TILES)
+        buf_ids[o] = jnp.zeros((8, TW), jnp.int32)
+        buf_ids[o, :, pl.ds(0, SLOTS)] = jnp.broadcast_to(ids, (8, SLOTS))
 
     sent, sent_y, sent_co, sent_ids = {}, {}, [], []
     todo = {}
@@ -150,8 +149,8 @@
     def later(t, work):
         todo.setdefault(t, []).append(work)
 
-    def to_core(t, oo, m, number):
-        copy = send(tasks(oo, m, number), to_co)
+    def to_core(t, oo, m, number, source=None):
+        copy = send(tasks(oo, m, number), to_co, source)
         other = oo + 1 - 2 * c
 
         def work():
@@ -183,11 +182,13 @@
                 copy.wait_send()
         if m < Y_OWN:
             right = left = tasks(o, m, 1)
+            source = ints.at[pl.ds(m * Y_TASKS, Y_TASKS)]
         else:
+            source = None
             right = tasks(line(yl, c), m - Y_OWN, 1)
             left = tasks(line(yr, c), Y_OWN // 2 + m - Y_OWN, 1)
         sent_y[m] = [
-            start(ref, device, y_send_sem.at[d, m % Y_SEND_AGAIN], y_recv_sem.at[d, m % Y_RECV_AGAIN])
+            start(ref, device, y_send_sem.at[d, m % Y_SEND_AGAIN], y_recv_sem.at[d, m % Y_RECV_AGAIN], source)
             for d, (ref, device) in enumerate(((right, to_yr), (left, to_yl)))
         ]
 
@@ -203,23 +204,27 @@
             for d in range(4):
                 if TABLE[d][t] >= 0:
                     p, zb, xb = place(TABLE[d][t])
+                    mine = amp.at[:, pl.ds(p * PT * TW, PT * TW)] if TABLE[d][t] % 64 == 0 else None
                     sent[t][d] = start(
-                        buf_a.at[p, zb, xb], to[d], send_sem.at[d, t % SEND_AGAIN], recv_sem.at[d, t % RECV_AGAIN]
+                        buf_a.at[p, zb, xb], to[d], send_sem.at[d, t % SEND_AGAIN], recv_sem.at[d, t % RECV_AGAIN], mine
                     )
         for m in range(Y_MSGS):
             if Y_STEP[m] == t:
                 y_send(m)
         if t == 0:
+            number_tasks()
             block = buf_ids.at[o]
             sent_ids = [send(block, to_yr), send(block, to_yl), send(block, to_co)]
             amp_hi[N_TILES] = jnp.zeros((PAIRS, TW), jnp.bfloat16)
             amp_lo[N_TILES] = jnp.zeros((PAIRS, TW), jnp.bfloat16)
-            total[...] = jnp.zeros_like(total)
+            for copy in own[4:]:
+                copy.wait()
             for p in range(PARTS):
                 convert_part(p, z, x)
         if t == 1:
             for q in range(0, Y_OWN, BATCH):
-                to_core(t, o, q, BATCH)
+                to_core(t, o, q, BATCH, ints.at[pl.ds(q * Y_TASKS, BATCH * Y_TASKS)])
+            own[3].wait()
             convert_groups(o, 0, SLOTS // GROUP)
         if t == LAG:
             sent_ids[0].wait_recv()
@@ -264,16 +269,11 @@
     def dot(a, b):
         return lax.dot_general(a, b, (((1,), (0,)), ((), ())), preferred_element_type=jnp.float32)
 
-    def product(h, carry):
-        g = DEPTH * h
-        a_hi = jnp.concatenate([tiles(amp_hi, g + j) for j in range(DEPTH)], axis=1)
-        a_lo = jnp.concatenate([tiles(amp_lo, g + j) for j in range(DEPTH)], axis=1)
-        b_hi = int_hi[pl.ds(g, DEPTH)].reshape(DEPTH * TW, GROUP * AB)
-        b_lo = int_lo[pl.ds(g, DEPTH)].reshape(DEPTH * TW, GROUP * AB)
-        total[...] += dot(a_hi, b_hi) + dot(a_lo, b_hi) + dot(a_hi, b_lo)
-        return carry
-
-    lax.fori_loop(0, N_GROUPS // DEPTH, product, 0)
+    a_hi = jnp.concatenate([tiles(amp_hi, g) for g in range(N_GROUPS)], axis=1)
+    a_lo = jnp.concatenate([tiles(amp_lo, g) for g in range(N_GROUPS)], axis=1)
+    b_hi = int_hi[...].reshape(N_GROUPS * TW, GROUP * AB)
+    b_lo = int_lo[...].reshape(N_GROUPS * TW, GROUP * AB)
+    total[...] = dot(a_hi, b_hi) + dot(a_lo, b_hi) + dot(a_hi, b_lo)
     result = total[pl.ds(0, PAIRS), pl.ds(0, AB)]
     for j in range(1, GROUP):
         result = result + total[pl.ds(j * PAIRS, PAIRS), pl.ds(j * AB, AB)]

time: 72.6 us -> 71.2 us (0.981)
  Pallas kernels: 70.5 us -> 69.1 us
    pallas_call x1, Pallas kernels: 70.5 us -> 69.1 us  [body(): pl.pallas_call(kernel, out_shape=jax.ShapeDtypeStruct((PAIRS, AB), f32),...]
where the time goes in v4:
time: 71.2 us; the launch traced here: 71.1 us
  Pallas kernels  69.1 us (97%)
  local copies, waits for them, and re-layouts  1.3 us (2%)
    pallas_call x1, Pallas kernels, body(): pl.pallas_call(kernel, out_shape=jax.ShapeDtypeStruct((PAIRS, AB), f32),...  69.1 us

profile of v4, /device:TPU:1, one launch (start us, length us, event | category | flops | bytes accessed | tf_op | source)
XLA Modules:
  0.0 71.1 jit_solution(11370273099511395547)
XLA Ops:
  0.7 69.1 %shard_map.55 = f32[16,32]{1,0:T(8,128)} custom-call(f32[16,2304]{1,0:T(8,128)} %amp.1, f32[64,32,128]{2,1,0:T(8,128)} %bitcast.3, s32[1,1]{1,0:T(1,128)S(6)} %copy.7.count_hbm, s32[1,64]{1,0:T(1,128)} %bitcast.4, s32[1,64]{1,0:T(1,128)} %bitcast.5), custom_call_target="tpu_custom_call" | custom-call | tf_op jit(solution)/shard_map/pallas_call | solution.py:289
  69.8 1.3 %copy.8 = f32[16,32]{1,0:T(8,128)} copy(f32[16,32]{1,0:T(8,128)} %shard_map.55) | data formatting | bytes 4096

commit v5 on v4

--- a/solution.py
+++ b/solution.py
@@ -19,29 +19,35 @@
 N_GROUPS = N_OCC * SLOTS // GROUP
 
 PARTS = 3
-LAGS = (3, 3, 3, 4, 4, 4, 5,)
+LAGS = (3, 3, 3, 4, 4, 5, 5, 5,)
 LAG = LAGS[-1]
 TABLE = (
-    (128, 64, 0, 144, 1, 143, 65, 129, 15, 130, 159, 14, 77, 18, 146, 67, 131, 30, 13, 76, 19, 147, 12, 4, 29, 84, 140, 28, 5, 74,
-     139, 69, 20, 6, 134, 155, 21, 9, 7, 71, 135, 22, 25, 136, 23, 100, 31, -1),
-    (64, 128, 0, 79, 112, 1, 48, 15, 78, 130, 127, 49, 77, 14, 190, 113, 67, 125, 3, 114, 189, 13, 12, 4, 75, 124, 188, 69, 11,
-     74, 5, 181, 10, 117, 59, 122, 70, 58, 9, 121, 7, 185, 183, 186, 120, 180, 129, -1),
-    (64, 0, 128, 112, 65, 129, 1, 160, 17, 49, 66, 130, 2, 113, 178, 18, 67, 3, 131, 179, 83, 68, 4, 132, 147, 98, 180, 5, 133,
-     69, 148, 181, 6, 134, 70, 53, 182, 165, 135, 101, 71, 183, 118, 25, 102, 85, 81, -1),
-    (64, 0, 128, 79, 176, 80, 15, 78, 143, 191, 95, 159, 14, 142, 77, 190, 158, 13, 141, 76, 125, 189, 12, 140, 75, 92, 188, 11,
-     28, 74, 108, 187, 10, 139, 122, 90, 186, 155, 138, 121, 89, 9, 25, 154, 57, 111, 169, 41),
+    (0, 128, 64, 16, 144, 1, 143, 14, 130, 78, 142, 2, 30, 3, 13, 67, 141, 4, 132, 76, 68, 157, 140, 147, 11, 133, 139, 10, 69,
+     91, 149, 74, 7, 135, 73, 71, 27, 25, 72, 89, 19, 158, 81, 175, 88, 23, 87, -1),
+    (64, 0, 128, 112, 79, 65, 129, 2, 14, 127, 142, 177, 66, 131, 77, 141, 3, 114, 76, 125, 68, 140, 11, 75, 60, 116, 52, 6, 134,
+     74, 70, 138, 54, 182, 187, 137, 135, 8, 136, 72, 185, 61, 1, 126, 184, 122, 183, 102),
+    (0, 128, 64, 1, 129, 65, 80, 2, 130, 32, 66, 177, 3, 131, 81, 67, 146, 4, 132, 179, 68, 51, 5, 133, 180, 69, 52, 6, 134, 20,
+     70, 100, 7, 135, 54, 118, 101, 33, 46, 151, 161, 144, 62, 36, 114, 41, 149, -1),
+    (0, 64, 128, 15, 79, 143, 16, 14, 78, 127, 142, 160, 13, 77, 62, 141, 94, 12, 76, 61, 140, 29, 11, 75, 92, 139, 188, 10, 74,
+     59, 138, 155, 26, 73, 58, 122, 154, 25, 100, 109, 173, 80, 165, 118, 41, 23, 171, -1),
 )
 STEPS = len(TABLE[0])
 PT = TPD // PARTS
+LATE_STEPS = 3
+LATE = ((1, 6), (2, 7), (2, 10))
+CAP = 2
+LATE_TASKS = CAP * len(LATE)
+LATE_GROUPS = N_OCC * LATE_TASKS // GROUP
 
 Y_TASKS = 4
 Y_OWN = SLOTS // Y_TASKS
 Y_MSGS = Y_OWN + Y_OWN // 2
 Y_STEP = [m * (STEPS - 12) // Y_MSGS for m in range(Y_MSGS)]
 BATCH = 4
-SEND_AGAIN, RECV_AGAIN = 7, 13
+SEND_AGAIN, RECV_AGAIN = 6, 12
 Y_SEND_AGAIN, Y_RECV_AGAIN = 6, 9
-SINGLES = 24
+SINGLES = 23
+LATE_READY = Y_STEP[-1] + 2 * LAG
 
 
 def lag(t):
@@ -49,7 +55,7 @@
 
 
 def kernel(amp, ints, count_hbm, owner_hbm, local_hbm, out, buf_a, buf_i, buf_ids, ids_s, count_s, owner_v, local_v,
-           amp_hi, amp_lo, int_hi, int_lo, total, own_sem, send_sem, recv_sem,
+           amp_hi, amp_lo, int_hi, int_lo, late_hi, late_lo, lists, late_task_s, late_tile_s, total, own_sem, send_sem, recv_sem,
            y_send_sem, y_recv_sem, one_send_sem, one_recv_sem):
     o, v = lax.axis_index("occ"), lax.axis_index("vir")
     y, c = o // 2, o % 2
@@ -117,7 +123,7 @@
             amp_lo[first + t] = lo
             return carry
 
-        lax.fori_loop(0, PT, one, 0)
+        lax.fori_loop(0, PT, one, 0, unroll=True)
 
     def convert_groups(oo, first, number):
         def one(j, carry):
@@ -192,7 +198,57 @@
             for d, (ref, device) in enumerate(((right, to_yr), (left, to_yl)))
         ]
 
-    for t in range(STEPS + 3 * LAG):
+    def list_tasks():
+        ids = jnp.concatenate([buf_ids[oo, pl.ds(0, 1), :] for oo in range(N_OCC)], axis=0)
+        lane = lax.broadcasted_iota(jnp.int32, (N_OCC, TW), 1)
+        early, late_task, late_tile = ids, jnp.zeros((N_OCC, TW), jnp.int32), jnp.full((N_OCC, TW), N_TILES, jnp.int32)
+        for j, (dx, dz) in enumerate(LATE):
+            first = ((x + NX - dx) % NX * NZ + (z + NZ - dz) % NZ) * TPD
+            named = (ids >= first) & (ids < first + TPD) & (lane < SLOTS)
+            early = jnp.where(named, N_TILES, early)
+            low = jnp.min(jnp.where(named, lane, TW), axis=1, keepdims=True)
+            high = jnp.max(jnp.where(named, lane, -1), axis=1, keepdims=True)
+            for r, (task, there) in enumerate(((low, low < TW), (high, high > low))):
+                tile = jnp.sum(jnp.where(named & (lane == task), ids, 0), axis=1, keepdims=True)
+                here = (lane == CAP * j + r) & there
+                late_task = jnp.where(here, task, late_task)
+                late_tile = jnp.where(here, tile, late_tile)
+        lists[0] = early
+        lists[1] = late_task
+        lists[2] = late_tile
+        loads = [
+            pltpu.make_async_copy(lists.at[n], ref, own_sem.at[n]) for n, ref in enumerate((ids_s, late_task_s, late_tile_s))
+        ]
+        for load in loads:
+            load.start()
+        for load in loads:
+            load.wait()
+
+    def late(ref, n):
+        return ref[n // LATE_TASKS, n % LATE_TASKS]
+
+    def list_late_groups():
+        for g in range(LATE_GROUPS):
+            rows = [buf_i[n // LATE_TASKS, late(late_task_s, n)] for n in range(g * GROUP, (g + 1) * GROUP)]
+            hi, lo = split(jnp.concatenate(rows, axis=0).T)
+            late_hi[g] = hi
+            late_lo[g] = lo
+
+    def dot(a, b):
+        return lax.dot_general(a, b, (((1,), (0,)), ((), ())), preferred_element_type=jnp.float32)
+
+    def product(tile_of, groups, b_hi, b_lo):
+        def side(ref):
+            return jnp.concatenate(
+                [jnp.concatenate([ref[tile_of(g * GROUP + j)] for j in range(GROUP)], axis=0) for g in range(groups)], axis=1
+            )
+
+        a_hi, a_lo = side(amp_hi), side(amp_lo)
+        b_hi = b_hi[...].reshape(groups * TW, GROUP * AB)
+        b_lo = b_lo[...].reshape(groups * TW, GROUP * AB)
+        return dot(a_hi, b_hi) + dot(a_lo, b_hi) + dot(a_hi, b_lo)
+
+    for t in range(STEPS + LAG):
         arrived = [s for s in range(STEPS) if s + lag(s) == t]
         for s in arrived:
             for copy in sent[s].values():
@@ -240,9 +296,7 @@
         if t == 3 * LAG:
             for copy in [sent_ids[2]] + sent_ids[4:]:
                 copy.wait_recv()
-            load = pltpu.make_async_copy(buf_ids, ids_s, own_sem.at[0])
-            load.start()
-            load.wait()
+            list_tasks()
         for m in range(Y_MSGS):
             if Y_STEP[m] + LAG == t:
                 y_arrived(t, m)
@@ -261,19 +315,12 @@
                     else:
                         zb = (zb + 1) % NZ
                     convert_part(p, zb, xb)
-
-    def tiles(ref, g):
-        oo, first = g // (SLOTS // GROUP), (g % (SLOTS // GROUP)) * GROUP
-        return jnp.concatenate([ref[ids_s[oo, 0, first + j]] for j in range(GROUP)], axis=0)
-
-    def dot(a, b):
-        return lax.dot_general(a, b, (((1,), (0,)), ((), ())), preferred_element_type=jnp.float32)
-
-    a_hi = jnp.concatenate([tiles(amp_hi, g) for g in range(N_GROUPS)], axis=1)
-    a_lo = jnp.concatenate([tiles(amp_lo, g) for g in range(N_GROUPS)], axis=1)
-    b_hi = int_hi[...].reshape(N_GROUPS * TW, GROUP * AB)
-    b_lo = int_lo[...].reshape(N_GROUPS * TW, GROUP * AB)
-    total[...] = dot(a_hi, b_hi) + dot(a_lo, b_hi) + dot(a_hi, b_lo)
+        if t == LATE_READY:
+            list_late_groups()
+        if t == STEPS - LATE_STEPS - 1 + LAG:
+            total[...] = product(lambda n: ids_s[n // SLOTS, n % SLOTS], N_GROUPS, int_hi, int_lo)
+
+    total[...] += product(lambda n: late(late_tile_s, n), LATE_GROUPS, late_hi, late_lo)
     result = total[pl.ds(0, PAIRS), pl.ds(0, AB)]
     for j in range(1, GROUP):
         result = result + total[pl.ds(j * PAIRS, PAIRS), pl.ds(j * AB, AB)]
@@ -295,7 +342,7 @@
             pltpu.VMEM((PARTS, NZ, NX, PAIRS, PT * TW), f32),
             pltpu.VMEM((N_OCC, SLOTS, AB, TW), f32),
             pltpu.VMEM((N_OCC, 8, TW), jnp.int32),
-            pltpu.SMEM((N_OCC, 8, TW), jnp.int32),
+            pltpu.SMEM((N_OCC, TW), jnp.int32),
             pltpu.SMEM((1, 1), jnp.int32),
             pltpu.VMEM((1, SLOTS), jnp.int32),
             pltpu.VMEM((1, SLOTS), jnp.int32),
@@ -303,6 +350,11 @@
             pltpu.VMEM((N_TILES + 1, PAIRS, TW), bf16),
             pltpu.VMEM((N_GROUPS, TW, GROUP * AB), bf16),
             pltpu.VMEM((N_GROUPS, TW, GROUP * AB), bf16),
+            pltpu.VMEM((LATE_GROUPS, TW, GROUP * AB), bf16),
+            pltpu.VMEM((LATE_GROUPS, TW, GROUP * AB), bf16),
+            pltpu.VMEM((3, N_OCC, TW), jnp.int32),
+            pltpu.SMEM((N_OCC, TW), jnp.int32),
+            pltpu.SMEM((N_OCC, TW), jnp.int32),
             pltpu.VMEM((GROUP * PAIRS, GROUP * AB), f32),
             pltpu.SemaphoreType.DMA((4 + PARTS,)),
             pltpu.SemaphoreType.DMA((4, SEND_AGAIN)),

time: 71.2 us -> 70 us (0.983); the launches traced: 71.1 us -> 69.1 us
  Pallas kernels: 69.1 us -> 67.1 us
    pallas_call x1, Pallas kernels: 69.1 us -> 67.1 us  [body(): pl.pallas_call(kernel, out_shape=jax.ShapeDtypeStruct((PAIRS, AB), f32),...]
where the time goes in v5:
time: 70 us; the launch traced here: 69.1 us
  Pallas kernels  67.1 us (96%)
  local copies, waits for them, and re-layouts  1.3 us (2%)
    pallas_call x1, Pallas kernels, body(): pl.pallas_call(kernel, out_shape=jax.ShapeDtypeStruct((PAIRS, AB), f32),...  67.1 us

profile of v5, /device:TPU:1, one launch (start us, length us, event | category | flops | bytes accessed | tf_op | source)
XLA Modules:
  0.0 69.1 jit_solution(3761326069408515248)
XLA Ops:
  0.7 67.1 %shard_map.55 = f32[16,32]{1,0:T(8,128)} custom-call(f32[16,2304]{1,0:T(8,128)} %amp.1, f32[64,32,128]{2,1,0:T(8,128)} %bitcast.3, s32[1,1]{1,0:T(1,128)S(6)} %copy.7.count_hbm, s32[1,64]{1,0:T(1,128)} %bitcast.4, s32[1,64]{1,0:T(1,128)} %bitcast.5), custom_call_target="tpu_custom_call" | custom-call | tf_op jit(solution)/shard_map/pallas_call | solution.py:336
  67.8 1.3 %copy.8 = f32[16,32]{1,0:T(8,128)} copy(f32[16,32]{1,0:T(8,128)} %shard_map.55) | data formatting | bytes 4096

commit v6 on v5

--- a/solution.py
+++ b/solution.py
@@ -47,7 +47,7 @@
 SEND_AGAIN, RECV_AGAIN = 6, 12
 Y_SEND_AGAIN, Y_RECV_AGAIN = 6, 9
 SINGLES = 23
-LATE_READY = Y_STEP[-1] + 2 * LAG
+LATE_READY = Y_STEP[-1] + 2 * LAG + 1
 
 
 def lag(t):
@@ -161,26 +161,32 @@
 
         def work():
             copy.wait_recv()
-            convert_groups(other, m * Y_TASKS // GROUP, number * Y_TASKS // GROUP)
+            convert_groups(other, m * Y_TASKS // GROUP, 1)
 
         later(t + LAG, work)
+        later(t + LAG + 1, lambda: convert_groups(other, m * Y_TASKS // GROUP + 1, 1))
 
     def y_arrived(t, m):
         for copy in sent_y[m]:
             copy.wait_recv()
         end = m + 1
+        pair = GROUP // Y_TASKS
+        if end % pair == 0:
+            if m < Y_OWN:
+                for yy in (yl, yr):
+                    convert_groups(line(yy, c), end // pair - 1, 1)
+            else:
+                for half in (0, Y_OWN // 2):
+                    convert_groups(line(yo, c), (half + end - Y_OWN) // pair - 1, 1)
         if end % BATCH:
             return
         first = end - BATCH
-        groups = BATCH * Y_TASKS // GROUP
         if m < Y_OWN:
             for yy in (yl, yr):
                 to_core(t, line(yy, c), first, BATCH)
-                convert_groups(line(yy, c), first * Y_TASKS // GROUP, groups)
         else:
             for half in (0, Y_OWN // 2):
                 to_core(t, line(yo, c), half + first - Y_OWN, BATCH)
-                convert_groups(line(yo, c), (half + first - Y_OWN) * Y_TASKS // GROUP, groups)
 
     def y_send(m):
         if m >= Y_SEND_AGAIN:
@@ -281,7 +287,8 @@
             for q in range(0, Y_OWN, BATCH):
                 to_core(t, o, q, BATCH, ints.at[pl.ds(q * Y_TASKS, BATCH * Y_TASKS)])
             own[3].wait()
-            convert_groups(o, 0, SLOTS // GROUP)
+        if 2 <= t < 2 + SLOTS // GROUP:
+            convert_groups(o, t - 2, 1)
         if t == LAG:
             sent_ids[0].wait_recv()
             sent_ids[1].wait_recv()

time: 70 us -> 70 us (level)
  no operation moved by 1% of the time
where the time goes in v6:
time: 70 us; the launch traced here: 69.1 us
  Pallas kernels  67.1 us (96%)
  local copies, waits for them, and re-layouts  1.3 us (2%)
    pallas_call x1, Pallas kernels, body(): pl.pallas_call(kernel, out_shape=jax.ShapeDtypeStruct((PAIRS, AB), f32),...  67.1 us

profile of v6, /device:TPU:1, one launch (start us, length us, event | category | flops | bytes accessed | tf_op | source)
XLA Modules:
  0.0 69.1 jit_solution(1795716733632962886)
XLA Ops:
  0.7 67.1 %shard_map.55 = f32[16,32]{1,0:T(8,128)} custom-call(f32[16,2304]{1,0:T(8,128)} %amp.1, f32[64,32,128]{2,1,0:T(8,128)} %bitcast.3, s32[1,1]{1,0:T(1,128)S(6)} %copy.7.count_hbm, s32[1,64]{1,0:T(1,128)} %bitcast.4, s32[1,64]{1,0:T(1,128)} %bitcast.5), custom_call_target="tpu_custom_call" | custom-call | tf_op jit(solution)/shard_map/pallas_call | solution.py:343
  67.8 1.3 %copy.8 = f32[16,32]{1,0:T(8,128)} copy(f32[16,32]{1,0:T(8,128)} %shard_map.55) | data formatting | bytes 4096
